TPU v7x, 32 devices: a whole 2x2x4 slice. The times are simulated.
32 devices in a mesh: arc: 8 (over y, x, core), mas: 4 (over z).
Axes of the slice: x: 2, y: 2, z: 4, core: 2. Of those that a mesh axis runs over, the one named last changes fastest.
Arguments:
- jac: bfloat16 [8, 16, 1024, 256], P('arc', 'mas')
- resid: float32 [8, 1024], P('arc'), may hold values from -6 to 6
- counts: int32 [8], P('arc'), may hold values from 512 to 1024
- vis: int32 [8, 16], P('arc'), may hold values from 0 to 39, as said below
- xcur: float32 [40, 256], P('mas'), may hold values from -6 to 6
- damp: float32 [40, 256], P('mas'), may hold values from 2 to 20
Outputs:
- updated: float32 [40, 256], P('mas')
- postfit: float32 [8, 1024], P('arc', 'mas')
Inputs may be any that keep to these rules, and one draw needn't show every extreme that they name: `vis`: each row names 16 distinct blocks; block b is held by index b // 10 of mas.
All inputs are finite; a program needn't handle non-finite values.
Results may differ from a plain program's by a relative error of at most 0.0003.
Values sent between devices are 32-bit elements; how exact they have to be, the bound alone decides.
A program may use at most 64 MiB of HBM per device.

v0:
```python
import jax
import jax.numpy as jnp
from jax import lax
from jax.sharding import PartitionSpec as P

ITERS = 4


def per_device(jac, resid, counts, vis, xcur, damp):
    mas_count = lax.axis_size("mas")
    mas_pos = lax.axis_index("mas")
    block_count = xcur.shape[0]
    slot_count = jac.shape[1]
    row_count = jac.shape[2]
    partials = jac[0]
    listed = vis[0]
    my_blocks = lax.dynamic_slice_in_dim(listed, mas_pos * slot_count, slot_count)
    valid_rows = jnp.arange(row_count) < counts[0]
    prefit = jnp.where(valid_rows, resid[0], 0.0)

    def spread(slot_terms):
        onehot = (my_blocks[:, None] == jnp.arange(block_count * mas_count)[None, :]).astype(
            jnp.float32
        )
        dense_sum = jnp.einsum("vn,vm->nm", onehot, slot_terms, precision=lax.Precision.HIGHEST)
        partial_sum = lax.psum_scatter(dense_sum, "mas", scatter_dimension=0, tiled=True)
        return lax.psum(partial_sum, "arc")

    def fetch(vector):
        gathered = lax.all_gather(vector, "mas", axis=0, tiled=True)
        return jnp.take(gathered, my_blocks, axis=0)

    def forward(slot_values):
        return jnp.einsum("vrm,vm->r", partials, slot_values, precision=lax.Precision.HIGHEST)

    def backward(row_values):
        return jnp.einsum("vrm,r->vm", partials, row_values, precision=lax.Precision.HIGHEST)

    def squares(remain):
        return lax.psum(jnp.sum(remain * remain), "mas")

    rhs = spread(backward(prefit))
    delta = jnp.zeros_like(rhs)
    remain = rhs
    direction = rhs
    norm_now = squares(remain)
    row_share = row_count // mas_count
    for iteration in range(ITERS):
        image_part = forward(fetch(direction))
        image_rows = jnp.where(valid_rows, lax.psum(image_part, "mas"), 0.0)
        applied = spread(backward(image_rows)) + damp * direction
        curvature = lax.psum(jnp.sum(direction * applied), "mas")
        step_len = norm_now / curvature
        delta = delta + step_len * direction
        remain = remain - step_len * applied
        norm_next = squares(remain)
        direction = remain + norm_next / norm_now * direction
        norm_now = norm_next
    change = forward(fetch(delta))
    post_sum = lax.psum_scatter(change[None, :], "mas", scatter_dimension=1, tiled=True)
    prefit_share = lax.dynamic_slice_in_dim(prefit, mas_pos * row_share, row_share)
    valid_share = lax.dynamic_slice_in_dim(valid_rows, mas_pos * row_share, row_share)
    postfit = jnp.where(valid_share, prefit_share - post_sum[0], 0.0)
    return (xcur + delta, postfit[None, :])


def solution(mesh):
    return jax.shard_map(
        per_device,
        mesh=mesh,
        in_specs=(
            P("arc", "mas", None, None),
            P("arc", None),
            P("arc"),
            P("arc", None),
            P("mas", None),
            P("mas", None),
        ),
        out_specs=(P("mas", None), P("arc", "mas")),
        check_vma=False,
    )
```

profile of v0, /device:TPU:0, one launch (start us, length us, event | category | flops | bytes accessed | tf_op | source)
XLA Modules:
  0.0 446.2 jit_solution(12359702845204120861)
XLA Ops:
  10.7 21.2 %all-reduce = f32[40,256]{1,0:T(8,128)S(1)} all-reduce(f32[40,256]{1,0:T(8,128)S(1)} %fusion.33), channel_id=2, replica_groups=mesh['arc'=8,'mas'=4] {'mas'}, use_global_device_ids=true, to_apply=%region_0.1.clone | all-reduce | flops 10240 | bytes 81920
  33.2 22.3 %psum.119 = f32[10,256]{1,0:T(8,128)S(1)} all-reduce(f32[10,256]{1,0:T(8,128)S(1)} %constant_dynamic-slice_fusion.4), channel_id=1, replica_groups=mesh['arc'=8,'mas'=4] {'arc'}, use_global_device_ids=true, to_apply=%region_1.2 | all-reduce | flops 2560 | bytes 20480 | tf_op jit(solution)/shard_map/psum | solution.py:27
  55.5 13.1 %all-gather = f32[4,10,256]{2,1,0:T(8,128)S(1)} all-gather(f32[1,10,256]{2,1,0:T(8,128)S(1)} %bitcast.95), channel_id=1, replica_groups=mesh['arc'=8,'mas'=4] {'mas'}, dimensions={0}, use_global_device_ids=true | all-gather | bytes 51200 | tf_op jit(solution)/shard_map/all_gather | solution.py:30
  71.0 8.5 %psum.121 = f32[1024]{0:T(1024)S(1)} all-reduce(f32[1024]{0:T(1024)S(1)} %bitcast.100), channel_id=1, replica_groups=mesh['arc'=8,'mas'=4] {'mas'}, use_global_device_ids=true, to_apply=%region_4.6 | all-reduce | flops 1024 | bytes 8192 | tf_op jit(solution)/shard_map/psum | solution.py:50
  80.7 17.9 %all-reduce.1 = f32[40,256]{1,0:T(8,128)S(1)} all-reduce(f32[40,256]{1,0:T(8,128)S(1)} %fusion.31), channel_id=3, replica_groups=mesh['arc'=8,'mas'=4] {'mas'}, use_global_device_ids=true, to_apply=%region_5.7.clone | all-reduce | flops 10240 | bytes 81920
  98.7 22.3 %psum.122 = f32[10,256]{1,0:T(8,128)S(1)} all-reduce(f32[10,256]{1,0:T(8,128)S(1)} %constant_dynamic-slice_fusion.3), channel_id=1, replica_groups=mesh['arc'=8,'mas'=4] {'arc'}, use_global_device_ids=true, to_apply=%region_6.8 | all-reduce | flops 2560 | bytes 20480 | tf_op jit(solution)/shard_map/psum | solution.py:27
  121.7 9.1 %all-reduce.5 = (f32[]{:T(128)}, f32[]{:T(128)}) all-reduce(f32[]{:T(128)} %get-tuple-element.4, f32[]{:T(128)} %get-tuple-element.3), channel_id=1, replica_groups=mesh['arc'=8,'mas'=4] {'mas'}, use_global_device_ids=true, to_apply=%region_3.4 | all-reduce | flops 2 | bytes 16 | tf_op jit(solution)/shard_map/psum | solution.py:40
  132.6 10.9 %psum.124 = f32[]{:T(128)} all-reduce(f32[]{:T(128)} %get-tuple-element.13), channel_id=1, replica_groups=mesh['arc'=8,'mas'=4] {'mas'}, use_global_device_ids=true, to_apply=%region_10.12 | all-reduce | flops 1 | bytes 8 | tf_op jit(solution)/shard_map/psum | solution.py:40
  144.8 13.2 %all-gather.1 = f32[4,10,256]{2,1,0:T(8,128)S(1)} all-gather(f32[1,10,256]{2,1,0:T(8,128)S(1)} %fusion.59), channel_id=1, replica_groups=mesh['arc'=8,'mas'=4] {'mas'}, dimensions={0}, use_global_device_ids=true | all-gather | bytes 51200 | tf_op jit(solution)/shard_map/all_gather | solution.py:30
  170.0 18.0 %all-reduce.2 = f32[40,256]{1,0:T(8,128)S(1)} all-reduce(f32[40,256]{1,0:T(8,128)S(1)} %fusion.29), channel_id=4, replica_groups=mesh['arc'=8,'mas'=4] {'mas'}, use_global_device_ids=true, to_apply=%region_12.14.clone | all-reduce | flops 10240 | bytes 81920
  188.0 22.3 %psum.126 = f32[10,256]{1,0:T(8,128)S(1)} all-reduce(f32[10,256]{1,0:T(8,128)S(1)} %constant_dynamic-slice_fusion.2), channel_id=1, replica_groups=mesh['arc'=8,'mas'=4] {'arc'}, use_global_device_ids=true, to_apply=%region_13.15 | all-reduce | flops 2560 | bytes 20480 | tf_op jit(solution)/shard_map/psum | solution.py:27
  211.0 9.1 %psum.127 = f32[]{:T(128)} all-reduce(f32[]{:T(128)} %multiply_reduce_fusion.4), channel_id=1, replica_groups=mesh['arc'=8,'mas'=4] {'mas'}, use_global_device_ids=true, to_apply=%region_15.17 | all-reduce | flops 1 | bytes 8 | tf_op jit(solution)/shard_map/psum | solution.py:52
  222.1 11.0 %psum.128 = f32[]{:T(128)} all-reduce(f32[]{:T(128)} %get-tuple-element.11), channel_id=1, replica_groups=mesh['arc'=8,'mas'=4] {'mas'}, use_global_device_ids=true, to_apply=%region_17.19 | all-reduce | flops 1 | bytes 8 | tf_op jit(solution)/shard_map/psum | solution.py:40
  234.3 13.1 %all-gather.2 = f32[4,10,256]{2,1,0:T(8,128)S(1)} all-gather(f32[1,10,256]{2,1,0:T(8,128)S(1)} %bitcast.96), channel_id=1, replica_groups=mesh['arc'=8,'mas'=4] {'mas'}, dimensions={0}, use_global_device_ids=true | all-gather | bytes 51200 | tf_op jit(solution)/shard_map/all_gather | solution.py:30
  259.4 18.0 %all-reduce.3 = f32[40,256]{1,0:T(8,128)S(1)} all-reduce(f32[40,256]{1,0:T(8,128)S(1)} %fusion.27), channel_id=5, replica_groups=mesh['arc'=8,'mas'=4] {'mas'}, use_global_device_ids=true, to_apply=%region_19.21.clone | all-reduce | flops 10240 | bytes 81920
  277.5 22.4 %psum.130 = f32[10,256]{1,0:T(8,128)S(1)} all-reduce(f32[10,256]{1,0:T(8,128)S(1)} %constant_dynamic-slice_fusion.1), channel_id=1, replica_groups=mesh['arc'=8,'mas'=4] {'arc'}, use_global_device_ids=true, to_apply=%region_20.22 | all-reduce | flops 2560 | bytes 20480 | tf_op jit(solution)/shard_map/psum | solution.py:27
  300.4 9.0 %psum.131 = f32[]{:T(128)} all-reduce(f32[]{:T(128)} %multiply_reduce_fusion.2), channel_id=1, replica_groups=mesh['arc'=8,'mas'=4] {'mas'}, use_global_device_ids=true, to_apply=%region_22.24 | all-reduce | flops 1 | bytes 8 | tf_op jit(solution)/shard_map/psum | solution.py:52
  311.3 11.0 %psum.132 = f32[]{:T(128)} all-reduce(f32[]{:T(128)} %get-tuple-element.9), channel_id=1, replica_groups=mesh['arc'=8,'mas'=4] {'mas'}, use_global_device_ids=true, to_apply=%region_24.26 | all-reduce | flops 1 | bytes 8 | tf_op jit(solution)/shard_map/psum | solution.py:40
  323.5 13.1 %all-gather.3 = f32[4,10,256]{2,1,0:T(8,128)S(1)} all-gather(f32[1,10,256]{2,1,0:T(8,128)S(1)} %fusion.51), channel_id=1, replica_groups=mesh['arc'=8,'mas'=4] {'mas'}, dimensions={0}, use_global_device_ids=true | all-gather | bytes 51200 | tf_op jit(solution)/shard_map/all_gather | solution.py:30
  348.6 18.0 %all-reduce.4 = f32[40,256]{1,0:T(8,128)S(1)} all-reduce(f32[40,256]{1,0:T(8,128)S(1)} %fusion.25), channel_id=6, replica_groups=mesh['arc'=8,'mas'=4] {'mas'}, use_global_device_ids=true, to_apply=%region_26.28.clone | all-reduce | flops 10240 | bytes 81920
  366.7 22.3 %psum.134 = f32[10,256]{1,0:T(8,128)S(1)} all-reduce(f32[10,256]{1,0:T(8,128)S(1)} %constant_dynamic-slice_fusion), channel_id=1, replica_groups=mesh['arc'=8,'mas'=4] {'arc'}, use_global_device_ids=true, to_apply=%region_27.29 | all-reduce | flops 2560 | bytes 20480 | tf_op jit(solution)/shard_map/psum | solution.py:27
  389.7 9.1 %psum.135 = f32[]{:T(128)} all-reduce(f32[]{:T(128)} %multiply_reduce_fusion), channel_id=1, replica_groups=mesh['arc'=8,'mas'=4] {'mas'}, use_global_device_ids=true, to_apply=%region_29.31 | all-reduce | flops 1 | bytes 8 | tf_op jit(solution)/shard_map/psum | solution.py:52
  400.7 13.1 %all-gather.4 = f32[4,10,256]{2,1,0:T(8,128)S(1)} all-gather(f32[1,10,256]{2,1,0:T(8,128)S(1)} %bitcast.98), channel_id=1, replica_groups=mesh['arc'=8,'mas'=4] {'mas'}, dimensions={0}, use_global_device_ids=true | all-gather | bytes 51200 | tf_op jit(solution)/shard_map/all_gather | solution.py:30
  417.1 20.6 %reduce-scatter.4.cloned.1.call-done = f32[256,1]{1,0:T(8,128)} async-done(((f32[1024,1]{1,0:T(8,128)}), f32[256,1]{1,0:T(8,128)}) %reduce-scatter.4.cloned.1.call-update) | async-done | bytes 1040
  (73 shorter events, 52.9 us)
Async XLA Ops:
  7.2 1.6 copy-start
  7.2 24.7 %copy-start.4 = (u32[32]{0:T(128)S(1)}, u32[32]{0:T(128)}, u32[]{:S(2)}) copy-start(u32[32]{0:T(128)} %constant.35) | copy-start | bytes 388
  7.2 430.5 %reduce-scatter.4.cloned.1.call-start = ((), (), s32[]{:S(2)}) async-start(), calls=%async_computation.1 | async-start | bytes 655360
  69.3 51.7 %copy-start.1 = (f32[10,256]{1,0:T(8,128)S(1)}, f32[10,256]{1,0:T(8,128)}, u32[]{:S(2)}) copy-start(f32[10,256]{1,0:T(8,128)} %param.13) | copy-start | bytes 30724
  337.3 62.8 %copy-start.3 = (f32[10,256]{1,0:T(8,128)S(1)}, f32[10,256]{1,0:T(8,128)}, u32[]{:S(2)}) copy-start(f32[10,256]{1,0:T(8,128)} %param.12) | copy-start | bytes 30724
  348.3 68.8 %copy-start.2 = (f32[1,1024]{1,0:T(1,128)S(1)}, f32[1,1024]{1,0:T(1,128)}, u32[]{:S(2)}) copy-start(f32[1,1024]{1,0:T(1,128)} %param.9) | copy-start | bytes 12292
Sparse Core Ops, SparseCore 0:
  417.2 20.4 reduce-scatter.3
where the time goes:
time: 447 us; the launch traced here: 446 us
  blocking collectives  373 us (83%)
  between operations  24.7 us (6%)
  waiting for transfers between devices  20.6 us (5%)
  matrix products  16.1 us (4%)
  other arithmetic  7.02 us (2%)
  local copies, waits for them, and re-layouts  4.5 us (1%)
    psum x5, blocking collectives, spread(): return lax.psum(partial_sum, 'arc')  112 us
    unnamed x5, blocking collectives  93.2 us
    all_gather x5, blocking collectives, fetch(): gathered = lax.all_gather(vector, 'mas', axis=0, tiled=True)  65.7 us
    psum x4, blocking collectives, squares(): return lax.psum(jnp.sum(remain * remain), 'mas')  41.9 us
    psum x4, blocking collectives, per_device(): image_rows = jnp.where(valid_rows, lax.psum(image_part, 'mas'), 0.0)  33.7 us
    psum x3, blocking collectives, per_device(): curvature = lax.psum(jnp.sum(direction * applied), 'mas')  27.1 us
    unnamed x2, waiting for transfers between devices  20.6 us
    dot_general x5, matrix products, forward(): jnp.einsum('vrm,vm->r', partials, slot_values, precision=lax.Precision.HI...  9.41 us
  transfers between devices with their start and end apart: 1, of which 1 were waited for; matrix products, arithmetic and copies ran while one was open for 0% of the time, Pallas kernels for 0%

commit v1 on v0

v1 whole, which is shorter than its diff:
```python
import functools

import jax
import jax.numpy as jnp
from jax import lax
from jax.experimental import pallas as pl
from jax.experimental.pallas import tpu as pltpu
from jax.sharding import PartitionSpec as P

ITERS = 4
LANES = 128
F32 = jnp.float32
BF16 = jnp.bfloat16
MESH = pl.DeviceIdType.MESH


def parts_of(x):
    hi = x.astype(BF16).astype(F32)
    rest = x - hi
    mid = rest.astype(BF16).astype(F32)
    return hi, mid, rest - mid


def split_rows(x):
    hi, mid, lo = parts_of(x)
    row = lax.broadcasted_iota(jnp.int32, (16, x.shape[1]), 0)
    zero = jnp.zeros((16, x.shape[1]), F32)
    stacked = jnp.where(row == 0, hi, jnp.where(row == 1, mid, jnp.where(row == 2, lo, zero)))
    return stacked.astype(BF16)


def total_of(x):
    return jnp.sum(jnp.sum(x, axis=0, keepdims=True), axis=1, keepdims=True)


def kernel(
    arcs, mas,
    counts, vis, jac_hbm, resid, xcur, damp,
    updated, postfit,
    jac, terms, images, damps, idrows, squares, field, picker, dampfield,
    jac_sem, z_send, z_recv, p_send, p_recv, a_send, a_recv, s_send, s_recv,
):
    arc = lax.axis_index("arc")
    pos = lax.axis_index("mas")
    slots, rows = jac.shape[0], jac.shape[1]
    held = damp.shape[0]
    blocks = held * mas
    halves = 2

    z_peers = [{"mas": lax.rem(pos + k, mas)} for k in range(1, mas)]
    p_peers = [{"arc": lax.rem(arc + k, arcs)} for k in range(1, arcs)]

    barrier = pltpu.get_barrier_semaphore()
    for peer in z_peers + p_peers:
        pl.semaphore_signal(barrier, inc=1, device_id=peer, device_id_type=MESH)

    loads = [
        pltpu.make_async_copy(jac_hbm.at[0, v], jac.at[v], jac_sem.at[v]) for v in range(slots)
    ]
    for load in loads:
        load.start()

    def push(peers, ref, send_sem, recv_sem):
        for peer in peers:
            pltpu.make_async_remote_copy(
                src_ref=ref, dst_ref=ref, send_sem=send_sem, recv_sem=recv_sem,
                device_id=peer, device_id_type=MESH,
            ).start()

    def take(ref, sem):
        pltpu.make_async_copy(ref, ref, sem).wait()

    valid = lax.broadcasted_iota(jnp.int32, (1, rows), 1) < counts[0]
    prefit = jnp.where(valid, resid[...], 0.0)

    lane_count = arcs * mas * halves * slots
    lane = lax.broadcasted_iota(jnp.int32, (1, lane_count), 1)
    per_dev = halves * slots
    slot_of = lax.rem(lane // per_dev, mas) * slots + lax.rem(lane, slots)
    named = jnp.zeros((1, lane_count), F32)
    for s in range(mas * slots):
        named = jnp.where(slot_of == s, vis[0, s].astype(F32), named)
    named = jnp.where(lane // (per_dev * mas) == arc, named, 0.0)
    idrows[arc] = named
    damps[pos] = damp[...]

    def backward(step, row_values, waits):
        w = split_rows(row_values)
        for v in range(slots):
            if waits:
                loads[v].wait()
            out = jnp.dot(w, jac[v], preferred_element_type=F32)
            out = jnp.sum(out[0:8], axis=0, keepdims=True)
            for h in range(halves):
                terms[step, arc, pos, pl.ds(h * slots + v, 1), :] = out[:, h * LANES:(h + 1) * LANES]

    def spread_start(step):
        push(z_peers, terms.at[step, arc, pos], z_send.at[step], z_recv.at[step])

    def spread_finish(step):
        take(terms.at[step, 0, pl.ds(0, mas - 1)], z_recv.at[step])
        push(p_peers, terms.at[step, arc], p_send.at[step], p_recv.at[step])

    def collect(step):
        take(terms.at[step, pl.ds(0, arcs - 1)], p_recv.at[step])
        every = terms[step].reshape(lane_count, LANES)
        chosen = picker[...]
        total = None
        for part in parts_of(every):
            add = jnp.dot(chosen, part.astype(BF16), preferred_element_type=F32)
            total = add if total is None else total + add
        return total

    def forward(step, direction):
        field[...] = direction
        image = None
        for v in range(slots):
            block = vis[0, pos * slots + v]
            value = jnp.concatenate(
                [field[pl.ds(block + h * blocks, 1), :] for h in range(halves)], axis=1
            )
            add = lax.dot_general(
                split_rows(value), jac[v], (((1,), (1,)), ((), ())), preferred_element_type=F32
            )
            image = add if image is None else image + add
        images[step, pos] = jnp.sum(image[0:8], axis=0, keepdims=True)
        push(z_peers, images.at[step, pos], a_send.at[step], a_recv.at[step])
        take(images.at[step, pl.ds(0, mas - 1)], a_recv.at[step])
        return jnp.where(valid, jnp.sum(images[step], axis=0), 0.0)

    backward(0, prefit, True)
    pl.semaphore_wait(barrier, mas + arcs - 2)
    spread_start(0)
    push(p_peers, idrows.at[arc], s_send.at[0], s_recv.at[0])
    push(z_peers, damps.at[pos], s_send.at[1], s_recv.at[1])
    spread_finish(0)

    take(idrows.at[pl.ds(0, arcs - 1)], s_recv.at[0])
    names = jnp.sum(idrows[...], axis=0).astype(jnp.int32)
    names = names + lax.rem(lane // slots, halves) * blocks
    target = lax.broadcasted_iota(jnp.int32, (halves * blocks, lane_count), 0)
    picker[...] = jnp.where(target == names, 1.0, 0.0).astype(BF16)
    take(damps.at[pl.ds(0, mas - 1)], s_recv.at[1])
    for k in range(mas):
        for h in range(halves):
            dampfield[pl.ds(h * blocks + k * held, held), :] = damps[k, :, h * LANES:(h + 1) * LANES]

    remain = collect(0)
    direction = remain
    norm_now = total_of(remain * remain)
    delta = jnp.zeros_like(remain)
    change = jnp.zeros((1, rows), F32)
    for step in range(ITERS):
        image = forward(step, direction)
        damped = dampfield[...] * direction
        if step < ITERS - 1:
            backward(step + 1, image, False)
            spread_start(step + 1)
            spread_finish(step + 1)
            applied = collect(step + 1) + damped
            step_len = norm_now / total_of(direction * applied)
            delta = delta + step_len * direction
            change = change + step_len * image
            remain = remain - step_len * applied
            norm_next = total_of(remain * remain)
            direction = remain + norm_next / norm_now * direction
            norm_now = norm_next
        else:
            power = image * image
            share = power[:, 0:LANES]
            for k in range(1, rows // LANES):
                share = share + power[:, k * LANES:(k + 1) * LANES]
            squares[arc] = share
            push(p_peers, squares.at[arc], s_send.at[2], s_recv.at[2])
            own = total_of(direction * damped)
            take(squares.at[pl.ds(0, arcs - 1)], s_recv.at[2])
            step_len = norm_now / (total_of(jnp.sum(squares[...], axis=0)) + own)
            delta = delta + step_len * direction
            change = change + step_len * image

    mine = jnp.zeros((held, LANES * halves), F32)
    for k in range(mas):
        piece = jnp.concatenate(
            [delta[h * blocks + k * held:h * blocks + (k + 1) * held, :] for h in range(halves)], axis=1
        )
        mine = jnp.where(pos == k, piece, mine)
    updated[...] = xcur[...] + mine
    share_rows = rows // mas
    after = prefit - change
    kept = jnp.zeros((1, share_rows), F32)
    for k in range(mas):
        kept = jnp.where(pos == k, after[:, k * share_rows:(k + 1) * share_rows], kept)
    postfit[...] = kept

    for step in range(ITERS):
        take(terms.at[step, 0, pl.ds(0, mas - 1)], z_send.at[step])
        take(terms.at[step, pl.ds(0, arcs - 1)], p_send.at[step])
        take(images.at[step, pl.ds(0, mas - 1)], a_send.at[step])
    take(idrows.at[pl.ds(0, arcs - 1)], s_send.at[0])
    take(damps.at[pl.ds(0, mas - 1)], s_send.at[1])
    take(squares.at[pl.ds(0, arcs - 1)], s_send.at[2])


def per_device(arcs, mas, jac, resid, counts, vis, xcur, damp):
    slots, rows, width = jac.shape[1:]
    held = damp.shape[0]
    blocks = held * mas
    lane_count = arcs * mas * 2 * slots
    smem = pl.BlockSpec(memory_space=pltpu.SMEM)
    vmem = pl.BlockSpec(memory_space=pltpu.VMEM)
    dma = pltpu.SemaphoreType.DMA
    return pl.pallas_call(
        functools.partial(kernel, arcs, mas),
        out_shape=(
            jax.ShapeDtypeStruct((held, width), F32),
            jax.ShapeDtypeStruct((1, rows // mas), F32),
        ),
        in_specs=[smem, smem, pl.BlockSpec(memory_space=pl.ANY), vmem, vmem, vmem],
        out_specs=(vmem, vmem),
        scratch_shapes=[
            pltpu.VMEM((slots, rows, width), BF16),
            pltpu.VMEM((ITERS, arcs, mas, 2 * slots, LANES), F32),
            pltpu.VMEM((ITERS, mas, 1, rows), F32),
            pltpu.VMEM((mas, held, width), F32),
            pltpu.VMEM((arcs, 1, lane_count), F32),
            pltpu.VMEM((arcs, 1, LANES), F32),
            pltpu.VMEM((2 * blocks, LANES), F32),
            pltpu.VMEM((2 * blocks, lane_count), BF16),
            pltpu.VMEM((2 * blocks, LANES), F32),
            dma((slots,)),
            dma((ITERS,)), dma((ITERS,)),
            dma((ITERS,)), dma((ITERS,)),
            dma((ITERS,)), dma((ITERS,)),
            dma((3,)), dma((3,)),
        ],
        compiler_params=pltpu.CompilerParams(
            collective_id=0, has_side_effects=True, vmem_limit_bytes=48 * 1024 * 1024
        ),
    )(counts, vis, jac, resid, xcur, damp)


def solution(mesh):
    return jax.shard_map(
        functools.partial(per_device, mesh.shape["arc"], mesh.shape["mas"]),
        mesh=mesh,
        in_specs=(
            P("arc", "mas", None, None),
            P("arc", None),
            P("arc"),
            P("arc", None),
            P("mas", None),
            P("mas", None),
        ),
        out_specs=(P("mas", None), P("arc", "mas")),
        check_vma=False,
    )
```

time: 447 us -> 63.9 us (0.14)
  blocking collectives: 373 us -> 0 us
  Pallas kernels: 0 us -> 56.7 us
  between operations: 24.7 us -> 1.3 us
  waiting for transfers between devices: 20.6 us -> 0 us
  matrix products: 16.1 us -> 0 us
  other arithmetic: 7.02 us -> 0 us
    psum x16 -> x0, blocking collectives: 214 us -> none  [the longest x5 112 us: spread(): return lax.psum(partial_sum, 'arc')]
    unnamed x5 -> x0, blocking collectives: 93.2 us -> none
    all_gather x5 -> x0, blocking collectives: 65.7 us -> none  [fetch(): gathered = lax.all_gather(vector, 'mas', axis=0, tiled=True)]
    pallas_call x0 -> x1, Pallas kernels: none -> 56.7 us  [per_device(): pl.pallas_call(functools.partial(kernel, arcs, mas), out_shape=(jax.Shape...]
    unnamed x2 -> x0, waiting for transfers between devices: 20.6 us -> none
    dot_general x15 -> x0, matrix products: 16.1 us -> none  [the longest x5 9.41 us: forward(): jnp.einsum('vrm,vm->r', partials, slot_values, precision=lax.Precision.HI...]
    reduce_sum x7 -> x0, other arithmetic: 4.58 us -> none  [the longest x4 2.67 us: per_device(): curvature = lax.psum(jnp.sum(direction * applied), 'mas')]
  transfers between devices with their start and end apart: 1 -> 0, of which waited for: 1 -> 0; matrix products, arithmetic and copies ran while one was open for 0% -> 0% of each run, Pallas kernels for 0% -> 0%
where the time goes in v1:
time: 63.9 us; the launch traced here: 63.5 us
  Pallas kernels  56.7 us (89%)
  local copies, waits for them, and re-layouts  5.53 us (9%)
  between operations  1.3 us (2%)
    pallas_call x1, Pallas kernels, per_device(): pl.pallas_call(functools.partial(kernel, arcs, mas), out_shape=(jax.Shape...  56.7 us
    unnamed x12, local copies, waits for them, and re-layouts  5.53 us

profile of v1, /device:TPU:0, one launch (start us, length us, event | category | flops | bytes accessed | tf_op | source)
XLA Modules:
  0.0 63.5 jit_solution(6568810956198266311)
XLA Ops:
  1.3 0.0 copy-start
  1.3 1.6 %copy-done = bf16[1,4,1024,256]{3,2,1,0:T(8,128)(2,1)S(1)} copy-done((bf16[1,4,1024,256]{3,2,1,0:T(8,128)(2,1)S(1)}, bf16[1,4,1024,256]{3,2,1,0:T(8,128)(2,1)}, u32[]{:S(2)}) %copy-start) | copy-done | bytes 2097176
  2.9 0.0 copy-start.1
  2.9 0.7 %copy-done.1 = f32[10,256]{1,0:T(8,128)S(1)} copy-done((f32[10,256]{1,0:T(8,128)S(1)}, f32[10,256]{1,0:T(8,128)}, u32[]{:S(2)}) %copy-start.1) | copy-done | bytes 10264
  3.6 0.0 copy-start.2
  3.6 0.7 %copy-done.2 = f32[10,256]{1,0:T(8,128)S(1)} copy-done((f32[10,256]{1,0:T(8,128)S(1)}, f32[10,256]{1,0:T(8,128)}, u32[]{:S(2)}) %copy-start.2) | copy-done | bytes 10264
  4.3 0.0 copy-start.3
  4.3 0.7 %copy-done.3 = f32[1,1024]{1,0:T(1,128)S(1)} copy-done((f32[1,1024]{1,0:T(1,128)S(1)}, f32[1,1024]{1,0:T(1,128)}, u32[]{:S(2)}) %copy-start.3) | copy-done | bytes 4120
  5.0 0.0 copy-start.4
  5.0 0.7 %copy-done.4 = s32[1,16]{1,0:T(1,128)S(1)} copy-done((s32[1,16]{1,0:T(1,128)S(1)}, s32[1,16]{1,0:T(1,128)}, u32[]{:S(2)}) %copy-start.4) | copy-done | bytes 88
  5.6 56.7 %shard_map.77 = (f32[10,256]{1,0:T(8,128)S(1)}, f32[1,256]{1,0:T(1,128)S(1)}) custom-call(s32[1]{0:T(128)S(6)} %copy.10.counts, s32[1,16]{1,0:T(1,128)S(1)} %copy-done.4, bf16[1,4,1024,256]{3,2,1,0:T(8,128)(2,1)S(1)} %copy-done, f32[1,1024]{1,0:T(1,128)S(1)} %copy-done.3, f32[10,256]{1,0:T(8,128)S(1)} %copy-done.1, f32[10,256]{1,0:T(8,128)S(1)} %copy-done.2), custom_call_target="tpu_custom_call" | custom-call | tf_op jit(solution)/shard_map/pallas_call | solution.py:212
  62.4 0.6 copy.11
  63.0 0.6 copy.12
Async XLA Ops:
  1.3 1.6 %copy-start = (bf16[1,4,1024,256]{3,2,1,0:T(8,128)(2,1)S(1)}, bf16[1,4,1024,256]{3,2,1,0:T(8,128)(2,1)}, u32[]{:S(2)}) copy-start(bf16[1,4,1024,256]{3,2,1,0:T(8,128)(2,1)} %jac_hbm.1) | copy-start | bytes 6291460
  2.9 0.7 %copy-start.1 = (f32[10,256]{1,0:T(8,128)S(1)}, f32[10,256]{1,0:T(8,128)}, u32[]{:S(2)}) copy-start(f32[10,256]{1,0:T(8,128)} %xcur.1) | copy-start | bytes 30724
  3.6 0.7 %copy-start.2 = (f32[10,256]{1,0:T(8,128)S(1)}, f32[10,256]{1,0:T(8,128)}, u32[]{:S(2)}) copy-start(f32[10,256]{1,0:T(8,128)} %damp.1) | copy-start | bytes 30724
  4.3 0.7 %copy-start.3 = (f32[1,1024]{1,0:T(1,128)S(1)}, f32[1,1024]{1,0:T(1,128)}, u32[]{:S(2)}) copy-start(f32[1,1024]{1,0:T(1,128)} %resid.1) | copy-start | bytes 12292
  5.0 0.7 %copy-start.4 = (s32[1,16]{1,0:T(1,128)S(1)}, s32[1,16]{1,0:T(1,128)}, u32[]{:S(2)}) copy-start(s32[1,16]{1,0:T(1,128)} %vis.1) | copy-start | bytes 196

commit v2 on v1

--- a/solution.py
+++ b/solution.py
@@ -35,29 +35,47 @@
 
 def kernel(
     arcs, mas,
-    counts, vis, jac_hbm, resid, xcur, damp,
+    counts, vis, jac_hbm, resid_hbm, xcur_hbm, damp_hbm,
     updated, postfit,
-    jac, terms, images, damps, idrows, squares, field, picker, dampfield,
-    jac_sem, z_send, z_recv, p_send, p_recv, a_send, a_recv, s_send, s_recv,
+    jac, resid, xcur, terms, images, damps, idrows, squares, field, picker, dampfield,
+    jac_sem, in_sem, p_send, p_recv, a_send, a_recv, s_send, s_recv,
 ):
     arc = lax.axis_index("arc")
     pos = lax.axis_index("mas")
     slots, rows = jac.shape[0], jac.shape[1]
-    held = damp.shape[0]
+    held = damp_hbm.shape[0]
     blocks = held * mas
     halves = 2
 
     z_peers = [{"mas": lax.rem(pos + k, mas)} for k in range(1, mas)]
     p_peers = [{"arc": lax.rem(arc + k, arcs)} for k in range(1, arcs)]
 
+    devices = arcs * mas
+    me = arc * mas + pos
+
+    def each_peer(act):
+        def one(k, carry):
+            other = lax.rem(me + k, devices)
+            act({"arc": other // mas, "mas": lax.rem(other, mas)})
+            return carry
+        if devices <= 32:
+            for k in range(1, devices):
+                one(k, 0)
+        else:
+            lax.fori_loop(1, devices, one, 0)
+
     barrier = pltpu.get_barrier_semaphore()
-    for peer in z_peers + p_peers:
-        pl.semaphore_signal(barrier, inc=1, device_id=peer, device_id_type=MESH)
+    each_peer(lambda peer: pl.semaphore_signal(barrier, inc=1, device_id=peer, device_id_type=MESH))
 
     loads = [
         pltpu.make_async_copy(jac_hbm.at[0, v], jac.at[v], jac_sem.at[v]) for v in range(slots)
     ]
-    for load in loads:
+    small = [
+        pltpu.make_async_copy(resid_hbm, resid, in_sem.at[0]),
+        pltpu.make_async_copy(xcur_hbm, xcur, in_sem.at[1]),
+        pltpu.make_async_copy(damp_hbm, damps.at[pos], in_sem.at[2]),
+    ]
+    for load in small + loads:
         load.start()
 
     def push(peers, ref, send_sem, recv_sem):
@@ -70,6 +88,7 @@
     def take(ref, sem):
         pltpu.make_async_copy(ref, ref, sem).wait()
 
+    small[0].wait()
     valid = lax.broadcasted_iota(jnp.int32, (1, rows), 1) < counts[0]
     prefit = jnp.where(valid, resid[...], 0.0)
 
@@ -82,7 +101,6 @@
         named = jnp.where(slot_of == s, vis[0, s].astype(F32), named)
     named = jnp.where(lane // (per_dev * mas) == arc, named, 0.0)
     idrows[arc] = named
-    damps[pos] = damp[...]
 
     def backward(step, row_values, waits):
         w = split_rows(row_values)
@@ -92,17 +110,14 @@
             out = jnp.dot(w, jac[v], preferred_element_type=F32)
             out = jnp.sum(out[0:8], axis=0, keepdims=True)
             for h in range(halves):
-                terms[step, arc, pos, pl.ds(h * slots + v, 1), :] = out[:, h * LANES:(h + 1) * LANES]
+                terms[step, me, pl.ds(h * slots + v, 1), :] = out[:, h * LANES:(h + 1) * LANES]
 
     def spread_start(step):
-        push(z_peers, terms.at[step, arc, pos], z_send.at[step], z_recv.at[step])
-
-    def spread_finish(step):
-        take(terms.at[step, 0, pl.ds(0, mas - 1)], z_recv.at[step])
-        push(p_peers, terms.at[step, arc], p_send.at[step], p_recv.at[step])
+        mine = terms.at[step, me]
+        each_peer(lambda peer: push([peer], mine, p_send.at[step], p_recv.at[step]))
 
     def collect(step):
-        take(terms.at[step, pl.ds(0, arcs - 1)], p_recv.at[step])
+        take(terms.at[step, pl.ds(0, devices - 1)], p_recv.at[step])
         every = terms[step].reshape(lane_count, LANES)
         chosen = picker[...]
         total = None
@@ -129,11 +144,11 @@
         return jnp.where(valid, jnp.sum(images[step], axis=0), 0.0)
 
     backward(0, prefit, True)
-    pl.semaphore_wait(barrier, mas + arcs - 2)
+    pl.semaphore_wait(barrier, devices - 1)
     spread_start(0)
     push(p_peers, idrows.at[arc], s_send.at[0], s_recv.at[0])
+    small[2].wait()
     push(z_peers, damps.at[pos], s_send.at[1], s_recv.at[1])
-    spread_finish(0)
 
     take(idrows.at[pl.ds(0, arcs - 1)], s_recv.at[0])
     names = jnp.sum(idrows[...], axis=0).astype(jnp.int32)
@@ -156,7 +171,6 @@
         if step < ITERS - 1:
             backward(step + 1, image, False)
             spread_start(step + 1)
-            spread_finish(step + 1)
             applied = collect(step + 1) + damped
             step_len = norm_now / total_of(direction * applied)
             delta = delta + step_len * direction
@@ -184,6 +198,7 @@
             [delta[h * blocks + k * held:h * blocks + (k + 1) * held, :] for h in range(halves)], axis=1
         )
         mine = jnp.where(pos == k, piece, mine)
+    small[1].wait()
     updated[...] = xcur[...] + mine
     share_rows = rows // mas
     after = prefit - change
@@ -193,8 +208,7 @@
     postfit[...] = kept
 
     for step in range(ITERS):
-        take(terms.at[step, 0, pl.ds(0, mas - 1)], z_send.at[step])
-        take(terms.at[step, pl.ds(0, arcs - 1)], p_send.at[step])
+        take(terms.at[step, pl.ds(0, devices - 1)], p_send.at[step])
         take(images.at[step, pl.ds(0, mas - 1)], a_send.at[step])
     take(idrows.at[pl.ds(0, arcs - 1)], s_send.at[0])
     take(damps.at[pl.ds(0, mas - 1)], s_send.at[1])
@@ -215,11 +229,13 @@
             jax.ShapeDtypeStruct((held, width), F32),
             jax.ShapeDtypeStruct((1, rows // mas), F32),
         ),
-        in_specs=[smem, smem, pl.BlockSpec(memory_space=pl.ANY), vmem, vmem, vmem],
+        in_specs=[smem, smem] + [pl.BlockSpec(memory_space=pl.ANY)] * 4,
         out_specs=(vmem, vmem),
         scratch_shapes=[
             pltpu.VMEM((slots, rows, width), BF16),
-            pltpu.VMEM((ITERS, arcs, mas, 2 * slots, LANES), F32),
+            pltpu.VMEM((1, rows), F32),
+            pltpu.VMEM((held, width), F32),
+            pltpu.VMEM((ITERS, arcs * mas, 2 * slots, LANES), F32),
             pltpu.VMEM((ITERS, mas, 1, rows), F32),
             pltpu.VMEM((mas, held, width), F32),
             pltpu.VMEM((arcs, 1, lane_count), F32),
@@ -228,13 +244,13 @@
             pltpu.VMEM((2 * blocks, lane_count), BF16),
             pltpu.VMEM((2 * blocks, LANES), F32),
             dma((slots,)),
-            dma((ITERS,)), dma((ITERS,)),
+            dma((3,)),
             dma((ITERS,)), dma((ITERS,)),
             dma((ITERS,)), dma((ITERS,)),
             dma((3,)), dma((3,)),
         ],
         compiler_params=pltpu.CompilerParams(
-            collective_id=0, has_side_effects=True, vmem_limit_bytes=48 * 1024 * 1024
+            collective_id=0, has_side_effects=True, vmem_limit_bytes=62 * 1024 * 1024
         ),
     )(counts, vis, jac, resid, xcur, damp)
 

time: 63.9 us -> 56.3 us (0.88)
  Pallas kernels: 56.7 us -> 52.2 us
  local copies, waits for them, and re-layouts: 5.53 us -> 2.54 us
    pallas_call x1, Pallas kernels: 56.7 us -> 52.2 us  [per_device(): pl.pallas_call(functools.partial(kernel, arcs, mas), out_shape=(jax.Shape...]
    unnamed x12 -> x2, local copies, waits for them, and re-layouts: 5.53 us -> 2.54 us
where the time goes in v2:
time: 56.3 us; the launch traced here: 56.1 us
  Pallas kernels  52.2 us (93%)
  local copies, waits for them, and re-layouts  2.54 us (5%)
  between operations  1.28 us (2%)
    pallas_call x1, Pallas kernels, per_device(): pl.pallas_call(functools.partial(kernel, arcs, mas), out_shape=(jax.Shape...  52.2 us
    unnamed x2, local copies, waits for them, and re-layouts  2.54 us

profile of v2, /device:TPU:0, one launch (start us, length us, event | category | flops | bytes accessed | tf_op | source)
XLA Modules:
  0.0 56.1 jit_solution(11244220154680118287)
XLA Ops:
  1.3 52.2 %shard_map.77 = (f32[10,256]{1,0:T(8,128)}, f32[1,256]{1,0:T(1,128)}) custom-call(s32[1]{0:T(128)S(6)} %copy.10.counts, s32[1,16]{1,0:T(1,128)} %vis.1, bf16[1,4,1024,256]{3,2,1,0:T(8,128)(2,1)} %jac_hbm.1, f32[1,1024]{1,0:T(1,128)} %resid_hbm.1, f32[10,256]{1,0:T(8,128)} %xcur_hbm.1, f32[10,256]{1,0:T(8,128)} %damp_hbm.1), custom_call_target="tpu_custom_call" | custom-call | tf_op jit(solution)/shard_map/pallas_call | solution.py:226
  53.5 1.3 %copy.11 = f32[10,256]{1,0:T(8,128)} copy(f32[10,256]{1,0:T(8,128)} %get-tuple-element.4) | data formatting | bytes 20480
  54.8 1.2 %copy.12 = f32[1,256]{1,0:T(1,128)} copy(f32[1,256]{1,0:T(1,128)} %get-tuple-element.5) | data formatting | bytes 2048

commit v3 on v2

--- a/solution.py
+++ b/solution.py
@@ -35,9 +35,9 @@
 
 def kernel(
     arcs, mas,
-    counts, vis, jac_hbm, resid_hbm, xcur_hbm, damp_hbm,
+    counts_hbm, vis_hbm, jac_hbm, resid_hbm, xcur_hbm, damp_hbm,
     updated, postfit,
-    jac, resid, xcur, terms, images, damps, idrows, squares, field, picker, dampfield,
+    counts, vis, jac, resid, xcur, terms, images, damps, idrows, everyone, field, picker, dampfield,
     jac_sem, in_sem, p_send, p_recv, a_send, a_recv, s_send, s_recv,
 ):
     arc = lax.axis_index("arc")
@@ -71,6 +71,8 @@
         pltpu.make_async_copy(jac_hbm.at[0, v], jac.at[v], jac_sem.at[v]) for v in range(slots)
     ]
     small = [
+        pltpu.make_async_copy(vis_hbm, vis, in_sem.at[3]),
+        pltpu.make_async_copy(counts_hbm, counts, in_sem.at[4]),
         pltpu.make_async_copy(resid_hbm, resid, in_sem.at[0]),
         pltpu.make_async_copy(xcur_hbm, xcur, in_sem.at[1]),
         pltpu.make_async_copy(damp_hbm, damps.at[pos], in_sem.at[2]),
@@ -88,7 +90,9 @@
     def take(ref, sem):
         pltpu.make_async_copy(ref, ref, sem).wait()
 
+    small[2].wait()
     small[0].wait()
+    small[1].wait()
     valid = lax.broadcasted_iota(jnp.int32, (1, rows), 1) < counts[0]
     prefit = jnp.where(valid, resid[...], 0.0)
 
@@ -138,7 +142,13 @@
                 split_rows(value), jac[v], (((1,), (1,)), ((), ())), preferred_element_type=F32
             )
             image = add if image is None else image + add
-        images[step, pos] = jnp.sum(image[0:8], axis=0, keepdims=True)
+        summed = jnp.sum(image[0:8], axis=0, keepdims=True)
+        if step == ITERS - 1:
+            everyone[me] = jnp.where(valid, summed, 0.0)
+            mine = everyone.at[me]
+            each_peer(lambda peer: push([peer], mine, s_send.at[2], s_recv.at[2]))
+            return None
+        images[step, pos] = summed
         push(z_peers, images.at[step, pos], a_send.at[step], a_recv.at[step])
         take(images.at[step, pl.ds(0, mas - 1)], a_recv.at[step])
         return jnp.where(valid, jnp.sum(images[step], axis=0), 0.0)
@@ -147,7 +157,7 @@
     pl.semaphore_wait(barrier, devices - 1)
     spread_start(0)
     push(p_peers, idrows.at[arc], s_send.at[0], s_recv.at[0])
-    small[2].wait()
+    small[4].wait()
     push(z_peers, damps.at[pos], s_send.at[1], s_recv.at[1])
 
     take(idrows.at[pl.ds(0, arcs - 1)], s_recv.at[0])
@@ -180,15 +190,15 @@
             direction = remain + norm_next / norm_now * direction
             norm_now = norm_next
         else:
-            power = image * image
-            share = power[:, 0:LANES]
-            for k in range(1, rows // LANES):
-                share = share + power[:, k * LANES:(k + 1) * LANES]
-            squares[arc] = share
-            push(p_peers, squares.at[arc], s_send.at[2], s_recv.at[2])
             own = total_of(direction * damped)
-            take(squares.at[pl.ds(0, arcs - 1)], s_recv.at[2])
-            step_len = norm_now / (total_of(jnp.sum(squares[...], axis=0)) + own)
+            take(everyone.at[pl.ds(0, devices - 1)], s_recv.at[2])
+            power = jnp.zeros((1, rows), F32)
+            image = jnp.zeros((1, rows), F32)
+            for k in range(arcs):
+                whole = jnp.sum(everyone[pl.ds(k * mas, mas)], axis=0)
+                power = power + whole * whole
+                image = jnp.where(arc == k, whole, image)
+            step_len = norm_now / (total_of(power) + own)
             delta = delta + step_len * direction
             change = change + step_len * image
 
@@ -198,7 +208,7 @@
             [delta[h * blocks + k * held:h * blocks + (k + 1) * held, :] for h in range(halves)], axis=1
         )
         mine = jnp.where(pos == k, piece, mine)
-    small[1].wait()
+    small[3].wait()
     updated[...] = xcur[...] + mine
     share_rows = rows // mas
     after = prefit - change
@@ -209,10 +219,11 @@
 
     for step in range(ITERS):
         take(terms.at[step, pl.ds(0, devices - 1)], p_send.at[step])
-        take(images.at[step, pl.ds(0, mas - 1)], a_send.at[step])
+        if step < ITERS - 1:
+            take(images.at[step, pl.ds(0, mas - 1)], a_send.at[step])
     take(idrows.at[pl.ds(0, arcs - 1)], s_send.at[0])
     take(damps.at[pl.ds(0, mas - 1)], s_send.at[1])
-    take(squares.at[pl.ds(0, arcs - 1)], s_send.at[2])
+    take(everyone.at[pl.ds(0, devices - 1)], s_send.at[2])
 
 
 def per_device(arcs, mas, jac, resid, counts, vis, xcur, damp):
@@ -220,7 +231,6 @@
     held = damp.shape[0]
     blocks = held * mas
     lane_count = arcs * mas * 2 * slots
-    smem = pl.BlockSpec(memory_space=pltpu.SMEM)
     vmem = pl.BlockSpec(memory_space=pltpu.VMEM)
     dma = pltpu.SemaphoreType.DMA
     return pl.pallas_call(
@@ -229,9 +239,11 @@
             jax.ShapeDtypeStruct((held, width), F32),
             jax.ShapeDtypeStruct((1, rows // mas), F32),
         ),
-        in_specs=[smem, smem] + [pl.BlockSpec(memory_space=pl.ANY)] * 4,
+        in_specs=[pl.BlockSpec(memory_space=pl.ANY)] * 6,
         out_specs=(vmem, vmem),
         scratch_shapes=[
+            pltpu.SMEM(counts.shape, jnp.int32),
+            pltpu.SMEM(vis.shape, jnp.int32),
             pltpu.VMEM((slots, rows, width), BF16),
             pltpu.VMEM((1, rows), F32),
             pltpu.VMEM((held, width), F32),
@@ -239,12 +251,12 @@
             pltpu.VMEM((ITERS, mas, 1, rows), F32),
             pltpu.VMEM((mas, held, width), F32),
             pltpu.VMEM((arcs, 1, lane_count), F32),
-            pltpu.VMEM((arcs, 1, LANES), F32),
+            pltpu.VMEM((arcs * mas, 1, rows), F32),
             pltpu.VMEM((2 * blocks, LANES), F32),
             pltpu.VMEM((2 * blocks, lane_count), BF16),
             pltpu.VMEM((2 * blocks, LANES), F32),
             dma((slots,)),
-            dma((3,)),
+            dma((5,)),
             dma((ITERS,)), dma((ITERS,)),
             dma((ITERS,)), dma((ITERS,)),
             dma((3,)), dma((3,)),

time: 56.3 us -> 54.5 us (0.968)
  Pallas kernels: 52.2 us -> 50.4 us
    pallas_call x1, Pallas kernels: 52.2 us -> 50.4 us  [per_device(): pl.pallas_call(functools.partial(kernel, arcs, mas), out_shape=(jax.Shape...]
where the time goes in v3:
time: 54.5 us; the launch traced here: 54.2 us
  Pallas kernels  50.4 us (92%)
  local copies, waits for them, and re-layouts  2.54 us (5%)
  between operations  1.28 us (2%)
    pallas_call x1, Pallas kernels, per_device(): pl.pallas_call(functools.partial(kernel, arcs, mas), out_shape=(jax.Shape...  50.4 us
    unnamed x2, local copies, waits for them, and re-layouts  2.54 us

profile of v3, /device:TPU:0, one launch (start us, length us, event | category | flops | bytes accessed | tf_op | source)
XLA Modules:
  0.0 54.2 jit_solution(6449335010854970786)
XLA Ops:
  1.3 50.4 %shard_map.77 = (f32[10,256]{1,0:T(8,128)}, f32[1,256]{1,0:T(1,128)}) custom-call(s32[1]{0:T(128)S(6)} %copy.10.counts_hbm, s32[1,16]{1,0:T(1,128)} %vis_hbm.1, bf16[1,4,1024,256]{3,2,1,0:T(8,128)(2,1)} %jac_hbm.1, f32[1,1024]{1,0:T(1,128)} %resid_hbm.1, f32[10,256]{1,0:T(8,128)} %xcur_hbm.1, f32[10,256]{1,0:T(8,128)} %damp_hbm.1), custom_call_target="tpu_custom_call" | custom-call | tf_op jit(solution)/shard_map/pallas_call | solution.py:236
  51.7 1.3 %copy.11 = f32[10,256]{1,0:T(8,128)} copy(f32[10,256]{1,0:T(8,128)} %get-tuple-element.4) | data formatting | bytes 20480
  53.0 1.2 %copy.12 = f32[1,256]{1,0:T(1,128)} copy(f32[1,256]{1,0:T(1,128)} %get-tuple-element.5) | data formatting | bytes 2048
